TPU v7x, 32 devices: a whole 2x2x4 slice. The times are simulated.
32 devices in a mesh: rep: 2 (over x), tile: 16 (over z, y, core).
Axes of the slice: x: 2, y: 2, z: 4, core: 2. Of those that a mesh axis runs over, the one named last changes fastest.
Arguments:
- mode_field: bfloat16 [120, 128, 32, 128], P(None, ('rep', 'tile')), parts along dimension 1, may hold values from -6 to 6
- conductivity: bfloat16 [36, 128, 32, 128], P(None, ('rep', 'tile')), parts along dimension 1, may hold values from -6 to 6
- triple_out: int32 [4096], replicated, may hold values from 0 to 119
- triple_in: int32 [4096], replicated, may hold values from 0 to 119
- triple_coef: int32 [4096], replicated, may hold values from 0 to 35
- triple_value: float32 [4096], replicated, may hold values from -1 to 1
Outputs:
- applied: bfloat16 [120, 128, 32, 128], P(None, ('rep', 'tile')), parts along dimension 1
There are 2 independent parts, one for each index of `rep`. A program takes and returns all parts, laid end to end along the dimension named above; an argument that names none is the same for every part. Nothing has to cross between parts.
Inputs may be any that keep to these rules, and one draw needn't show every extreme that they name: triple_out, triple_in and triple_coef at the same position name one coupling; repeated couplings add.
All inputs are finite; a program needn't handle non-finite values.
Results may differ from a plain program's by a relative error of at most 0.0057.
Values may be sent and summed in bfloat16 or wider, within the bound.
A program may use at most 64 MiB of HBM per device.

v0:
```python
import functools
import jax
import jax.numpy as jnp
from jax import lax
from jax.experimental import pallas as pl
from jax.experimental.pallas import tpu as pltpu
from jax.sharding import PartitionSpec as P

LANES = 128
COPIES = 4


def coupling_kernel(coefs, modes, row_ref, in_ref, value_ref, out_ref, *sums):
    for s in sums:
        s[...] = jnp.zeros_like(s)
    lane = lax.broadcasted_iota(jnp.int32, (1, LANES), 1)
    n = row_ref.shape[0]

    def step(t, carry):
        for u in range(4):
            for c in range(COPIES):
                at = t * (4 * COPIES) + u * COPIES + c
                row = row_ref[at]
                hit = jnp.where(lane == in_ref[at], value_ref[at], 0.0)
                sums[c][pl.ds(row, 1), :] += hit
        return carry

    lax.fori_loop(0, n // (4 * COPIES), step, 0)
    for k in range(coefs):
        rows = pl.ds(k * LANES, LANES)
        total = sums[0][rows, :]
        for c in range(1, COPIES):
            total = total + sums[c][rows, :]
        out_ref[:, k * LANES : (k + 1) * LANES] = total[:modes].astype(jnp.bfloat16)


def coupling_matrix(triple_out, triple_in, triple_coef, triple_value, modes, coefs):
    rows = triple_coef * LANES + triple_out
    smem = pl.BlockSpec(memory_space=pltpu.SMEM)
    return pl.pallas_call(
        functools.partial(coupling_kernel, coefs, modes),
        out_shape=jax.ShapeDtypeStruct((modes, coefs * LANES), jnp.bfloat16),
        in_specs=[smem] * 3,
        out_specs=pl.BlockSpec(memory_space=pltpu.VMEM),
        scratch_shapes=[pltpu.VMEM((coefs * LANES, LANES), jnp.float32)] * COPIES,
        cost_estimate=pl.CostEstimate(flops=40_000_000, bytes_accessed=40_000_000, transcendentals=0),
        compiler_params=pltpu.CompilerParams(vmem_limit_bytes=40 << 20),
    )(rows, triple_in, triple_value)


def main_kernel(coefs, modes, depth, rows, c_ref, m_ref, k_ref, o_ref, dm, kf, kb, terms):
    lane = lax.broadcasted_iota(jnp.int32, (1, LANES), 1)

    def shifted(v):
        before = jnp.where(lane == 0, 0.0, pltpu.roll(v, 1, 1))
        after = jnp.where(lane == LANES - 1, 0.0, pltpu.roll(v, LANES - 1, 1))
        return before, after

    def around(ref, z, y):
        f32 = jnp.float32
        center = ref[z, y].astype(f32)
        return center, (
            ref[z - 1, y].astype(f32),
            ref[z + 1, y].astype(f32),
            ref[z, y - 1].astype(f32),
            ref[z, y + 1].astype(f32),
        ) + shifted(center)

    def prepare(z, y, r):
        center, near = around(m_ref, z, y)
        for d in range(6):
            dm[r, d] = (center - near[d]).astype(jnp.bfloat16)
        center, near = around(k_ref, z, y)
        for d in range(6):
            kf[r, d] = 0.5 * (center + near[d])
        for d in range(6):
            for k in range(coefs):
                row = jnp.broadcast_to(kf[r, d, k : k + 1, :], (16, LANES))
                kb[r, d, k] = row.astype(jnp.bfloat16)

    def fill(slot):
        for r in range(2):
            for jg in range(LANES // 64):
                parts = [[dm[r, d, jg * 64 + 16 * q : jg * 64 + 16 * q + 16, :] for q in range(4)] for d in range(6)]
                for k in range(coefs):
                    face = [kb[r, d, k] for d in range(6)]
                    for q in range(4):
                        p = [face[d] * parts[d][q] for d in range(6)]
                        t = (p[0] + p[1]) + (p[2] + p[3]) + (p[4] + p[5])
                        at = k * LANES + jg * 64 + 16 * q
                        terms[slot, at : at + 16, r * LANES : (r + 1) * LANES] = t

    def place(s):
        pairs = rows // 2
        return s // pairs + 1, s % pairs * 2 + 1

    def multiply(s, slot):
        z, y = place(s)
        got = jnp.dot(c_ref[...], terms[slot], preferred_element_type=jnp.float32)
        for r in range(2):
            o_ref[z - 1, y - 1 + r] = got[:, r * LANES : (r + 1) * LANES].astype(jnp.bfloat16)

    def ready(s, slot):
        z, y = place(s)
        for r in range(2):
            prepare(z, y + r, r)
        fill(slot)

    total = depth * rows // 2
    ready(0, 0)

    def step(h, carry):
        s = h * 2
        ready(s + 1, 1)
        multiply(s, 0)
        ready(jnp.minimum(s + 2, total - 1), 0)
        multiply(s + 1, 1)
        return carry

    lax.fori_loop(0, total // 2, step, 0)


def per_device(mode_field, conductivity, triple_out, triple_in, triple_coef, triple_value):
    modes, depth, rows, lanes = mode_field.shape
    coefs = conductivity.shape[0]
    coefs_pad = -(-coefs // 16) * 16
    coupling = coupling_matrix(triple_out, triple_in, triple_coef, triple_value, modes, coefs)
    devices = lax.axis_size("tile")
    up = [(i, i + 1) for i in range(devices - 1)]
    down = [(j, i) for i, j in up]

    def extend(shard, pad):
        before = lax.ppermute(shard[:, -1:], "tile", up)
        after = lax.ppermute(shard[:, :1], "tile", down)
        whole = jnp.concatenate([before, shard, after], axis=1)
        whole = jnp.transpose(whole, (1, 2, 0, 3))
        return jnp.pad(whole, ((0, 0), (1, 1), (0, pad), (0, 0)))

    m_ext = extend(mode_field, LANES - modes)
    k_ext = extend(conductivity, coefs_pad - coefs)
    vmem = pl.BlockSpec(memory_space=pltpu.VMEM)
    out = pl.pallas_call(
        functools.partial(main_kernel, coefs, modes, depth, rows),
        out_shape=jax.ShapeDtypeStruct((depth, rows, modes, lanes), jnp.bfloat16),
        in_specs=[vmem] * 3,
        out_specs=vmem,
        scratch_shapes=[
            pltpu.VMEM((2, 6, LANES, LANES), jnp.bfloat16),
            pltpu.VMEM((2, 6, coefs_pad, LANES), jnp.float32),
            pltpu.VMEM((2, 6, coefs, 16, LANES), jnp.bfloat16),
            pltpu.VMEM((2, coefs * LANES, 2 * LANES), jnp.bfloat16),
        ],
        compiler_params=pltpu.CompilerParams(vmem_limit_bytes=48 << 20),
    )(coupling, m_ext, k_ext)
    return jnp.transpose(out, (2, 0, 1, 3))


def solution(mesh):
    return jax.shard_map(
        per_device,
        mesh=mesh,
        in_specs=(
            P(None, ("rep", "tile"), None, None),
            P(None, ("rep", "tile"), None, None),
            P(),
            P(),
            P(),
            P(),
        ),
        out_specs=P(None, ("rep", "tile"), None, None),
        check_vma=False,
    )
```

profile of v0, /device:TPU:25, one launch (start us, length us, event | category | flops | bytes accessed | tf_op | source)
XLA Modules:
  0.0 226.6 jit_solution(13540631351977730096)
XLA Ops:
  0.0 4.6 %copy.7 = bf16[120,4,32,128]{3,0,2,1:T(8,128)(2,1)S(1)} copy(bf16[120,4,32,128]{3,2,1,0:T(8,128)(2,1)} %param.6) | data formatting | bytes 7864320 | tf_op args[0]
  4.6 0.0 copy-start.2
  4.7 0.0 copy-start.3
  4.7 0.0 copy-start.4
  4.7 0.0 copy-start
  4.7 0.0 copy-start.1
  4.7 0.1 fusion
  4.9 3.8 %collective-permute-start = (bf16[120,1,32,128]{3,0,2,1:T(8,128)(2,1)S(1)}, bf16[120,1,32,128]{3,0,2,1:T(8,128)(2,1)S(1)}, u32[]{:S(2)}, u32[]{:S(2)}) collective-permute-start(bf16[120,1,32,128]{3,0,2,1:T(8,128)(2,1)S(1)} %get-tuple-element.5), channel_id=1, source_target_pairs={{0,1},{1,2},{2,3},{3,4},{4,5},{5,6},{6,7},{7,8},{8,9},{9,10},{10,1... | collective-permute-start | bytes 2949128 | tf_op jit(solution)/shard_map/ppermute | solution.py:133
  8.7 1.9 collective-permute-start.1
  10.6 0.0 copy-done.2
  10.6 0.8 copy.10
  11.4 0.1 fusion.1
  11.5 3.6 %collective-permute-start.2 = (bf16[36,1,32,128]{3,0,2,1:T(8,128)(2,1)S(1)}, bf16[36,1,32,128]{3,0,2,1:T(8,128)(2,1)S(1)}, u32[]{:S(2)}, u32[]{:S(2)}) collective-permute-start(bf16[36,1,32,128]{3,0,2,1:T(8,128)(2,1)S(1)} %get-tuple-element.7), channel_id=1, source_target_pairs={{0,1},{1,2},{2,3},{3,4},{4,5},{5,6},{6,7},{7,8},{8,9},{9,10},{10,1... | collective-permute-start | bytes 884744 | tf_op jit(solution)/shard_map/ppermute | solution.py:133
  15.1 2.1 collective-permute-start.3
  17.3 0.0 copy-done.3
  17.3 0.0 copy-done.4
  17.3 0.0 copy-done
  17.3 0.0 copy-done.1
  17.3 10.3 %shard_map.64.c_ref = bf16[120,4608]{1,0:T(8,128)(2,1)S(1)} custom-call(s32[4096]{0:T(1024)S(1)} %multiply_add_fusion.row_ref, s32[4096]{0:T(1024)S(1)} %copy-done, f32[4096]{0:T(1024)S(1)} %copy-done.1), custom_call_target="tpu_custom_call" | custom-call | flops 40000000 | bytes 40000000 | tf_op jit(solution)/shard_map/pallas_call | solution.py:40
  27.6 0.0 collective-permute-done.2
  27.6 11.2 %collective-permute-done.3 = bf16[36,1,32,128]{3,0,2,1:T(8,128)(2,1)S(1)} collective-permute-done((bf16[36,1,32,128]{3,0,2,1:T(8,128)(2,1)S(1)}, bf16[36,1,32,128]{3,0,2,1:T(8,128)(2,1)S(1)}, u32[]{:S(2)}, u32[]{:S(2)}) %collective-permute-start.3) | collective-permute-done | bytes 294944 | tf_op jit(solution)/shard_map/ppermute | solution.py:134
  38.8 0.3 maximum_bitcast_fusion.1
  39.1 0.4 pad.9.k_ref
  39.5 0.0 collective-permute-done
  39.5 0.0 collective-permute-done.1
  39.5 0.9 maximum_bitcast_fusion
  40.4 4.6 %pad.8.m_ref = bf16[6,34,128,128]{3,2,1,0:T(8,128)(2,1)} pad(bf16[6,32,120,128]{3,2,1,0:T(8,128)(2,1)S(1)} %maximum_bitcast_fusion, bf16[]{:T(256)} %constant.4.clone.1), padding=0_0x1_1x0_8x0_0 | pad | bytes 12582914 | tf_op jit(solution)/shard_map/jit(_pad)/pad | solution.py:137
  45.1 176.5 %shard_map.65 = bf16[4,32,120,128]{3,2,1,0:T(8,128)(2,1)} custom-call(bf16[120,4608]{1,0:T(8,128)(2,1)S(1)} %shard_map.64.c_ref, bf16[6,34,128,128]{3,2,1,0:T(8,128)(2,1)} %pad.8.m_ref, bf16[6,34,48,128]{3,2,1,0:T(8,128)(2,1)S(1)} %pad.9.k_ref), custom_call_target="tpu_custom_call" | custom-call | tf_op jit(solution)/shard_map/pallas_call | solution.py:142
  221.6 5.1 %copy.13 = bf16[120,4,32,128]{3,2,1,0:T(8,128)(2,1)} copy(bf16[120,4,32,128]{3,0,2,1:T(8,128)(2,1)} %bitcast.5) | data formatting | bytes 7864320 | tf_op jit(solution)/shard_map/transpose | solution.py:155
  (1 shorter events, 0.0 us)
Async XLA Ops:
  4.6 6.0 %copy-start.2 = (bf16[36,4,32,128]{3,2,1,0:T(8,128)(2,1)S(1)}, bf16[36,4,32,128]{3,2,1,0:T(8,128)(2,1)}, u32[]{:S(2)}) copy-start(bf16[36,4,32,128]{3,2,1,0:T(8,128)(2,1)} %param.7) | copy-start | bytes 3538948
  4.7 12.6 %copy-start.3 = (s32[4096]{0:T(1024)S(1)}, s32[4096]{0:T(1024)}, u32[]{:S(2)}) copy-start(s32[4096]{0:T(1024)} %param.8) | copy-start | bytes 49156
  4.7 12.6 %copy-start.4 = (s32[4096]{0:T(1024)S(1)}, s32[4096]{0:T(1024)}, u32[]{:S(2)}) copy-start(s32[4096]{0:T(1024)} %param.10) | copy-start | bytes 49156
  4.7 12.6 %copy-start = (s32[4096]{0:T(1024)S(1)}, s32[4096]{0:T(1024)}, u32[]{:S(2)}) copy-start(s32[4096]{0:T(1024)} %in_ref.1) | copy-start | bytes 49156
  4.7 12.6 %copy-start.1 = (f32[4096]{0:T(1024)S(1)}, f32[4096]{0:T(1024)}, u32[]{:S(2)}) copy-start(f32[4096]{0:T(1024)} %value_ref.1) | copy-start | bytes 49156
  4.9 34.7 %collective-permute-start = (bf16[120,1,32,128]{3,0,2,1:T(8,128)(2,1)S(1)}, bf16[120,1,32,128]{3,0,2,1:T(8,128)(2,1)S(1)}, u32[]{:S(2)}, u32[]{:S(2)}) collective-permute-start(bf16[120,1,32,128]{3,0,2,1:T(8,128)(2,1)S(1)} %get-tuple-element.5), channel_id=1, source_target_pairs={{0,1},{1,2},{2,3},{3,4},{4,5},{5,6},{6,7},{7,8},{8,9},{9,10},{10,1... | collective-permute-start | bytes 2949128 | tf_op jit(solution)/shard_map/ppermute | solution.py:133
  8.7 30.8 %collective-permute-start.1 = (bf16[120,1,32,128]{3,0,2,1:T(8,128)(2,1)S(1)}, bf16[120,1,32,128]{3,0,2,1:T(8,128)(2,1)S(1)}, u32[]{:S(2)}, u32[]{:S(2)}) collective-permute-start(bf16[120,1,32,128]{3,0,2,1:T(8,128)(2,1)S(1)} %get-tuple-element.6), channel_id=1, source_target_pairs={{1,0},{2,1},{3,2},{4,3},{5,4},{6,5},{7,6},{8,7},{9,8},{10,9},{11,1... | collective-permute-start | bytes 2949128 | tf_op jit(solution)/shard_map/ppermute | solution.py:134
  11.5 16.1 %collective-permute-start.2 = (bf16[36,1,32,128]{3,0,2,1:T(8,128)(2,1)S(1)}, bf16[36,1,32,128]{3,0,2,1:T(8,128)(2,1)S(1)}, u32[]{:S(2)}, u32[]{:S(2)}) collective-permute-start(bf16[36,1,32,128]{3,0,2,1:T(8,128)(2,1)S(1)} %get-tuple-element.7), channel_id=1, source_target_pairs={{0,1},{1,2},{2,3},{3,4},{4,5},{5,6},{6,7},{7,8},{8,9},{9,10},{10,1... | collective-permute-start | bytes 884744 | tf_op jit(solution)/shard_map/ppermute | solution.py:133
  15.1 23.7 %collective-permute-start.3 = (bf16[36,1,32,128]{3,0,2,1:T(8,128)(2,1)S(1)}, bf16[36,1,32,128]{3,0,2,1:T(8,128)(2,1)S(1)}, u32[]{:S(2)}, u32[]{:S(2)}) collective-permute-start(bf16[36,1,32,128]{3,0,2,1:T(8,128)(2,1)S(1)} %get-tuple-element.8), channel_id=1, source_target_pairs={{1,0},{2,1},{3,2},{4,3},{5,4},{6,5},{7,6},{8,7},{9,8},{10,9},{11,1... | collective-permute-start | bytes 884744 | tf_op jit(solution)/shard_map/ppermute | solution.py:134
where the time goes:
time: 227 us
  Pallas kernels  187 us (82%)
  local copies, waits for them, and re-layouts  15.8 us (7%)
  starting transfers between devices  11.5 us (5%)
  waiting for transfers between devices  11.3 us (5%)
    pallas_call x1, Pallas kernels, per_device(): pl.pallas_call(functools.partial(main_kernel, coefs, modes, depth, rows),...  177 us
    ppermute x2, waiting for transfers between devices, extend(): after = lax.ppermute(shard[:, :1], 'tile', down)  11.2 us
    pallas_call x1, Pallas kernels, coupling_matrix(): pl.pallas_call(functools.partial(coupling_kernel, coefs, modes), out_shap...  10.3 us
    ppermute x2, starting transfers between devices, extend(): before = lax.ppermute(shard[:, -1:], 'tile', up)  7.48 us
    unnamed x12, local copies, waits for them, and re-layouts  5.45 us
    transpose x1, local copies, waits for them, and re-layouts, per_device(): return jnp.transpose(out, (2, 0, 1, 3))  5.06 us
    pad x2, local copies, waits for them, and re-layouts, extend(): return jnp.pad(whole, ((0, 0), (1, 1), (0, pad), (0, 0)))  5.05 us
  transfers between devices with their start and end apart: 4, of which 1 were waited for; matrix products, arithmetic and copies ran while one was open for 1% of the time, Pallas kernels for 5%

commit v1 on v0

--- a/solution.py
+++ b/solution.py
@@ -8,6 +8,7 @@
 
 LANES = 128
 COPIES = 4
+GROUP = 6
 
 
 def coupling_kernel(coefs, modes, row_ref, in_ref, value_ref, out_ref, *sums):
@@ -78,46 +79,47 @@
                 row = jnp.broadcast_to(kf[r, d, k : k + 1, :], (16, LANES))
                 kb[r, d, k] = row.astype(jnp.bfloat16)
 
-    def fill(slot):
+    def fill(slot, g):
+        base = pl.multiple_of(g * (GROUP * LANES), GROUP * LANES)
         for r in range(2):
             for jg in range(LANES // 64):
                 parts = [[dm[r, d, jg * 64 + 16 * q : jg * 64 + 16 * q + 16, :] for q in range(4)] for d in range(6)]
-                for k in range(coefs):
-                    face = [kb[r, d, k] for d in range(6)]
+                for k in range(GROUP):
+                    face = [kb[r, d, g * GROUP + k] for d in range(6)]
                     for q in range(4):
                         p = [face[d] * parts[d][q] for d in range(6)]
                         t = (p[0] + p[1]) + (p[2] + p[3]) + (p[4] + p[5])
                         at = k * LANES + jg * 64 + 16 * q
-                        terms[slot, at : at + 16, r * LANES : (r + 1) * LANES] = t
+                        terms[slot, pl.ds(base + at, 16), r * LANES : (r + 1) * LANES] = t
 
     def place(s):
         pairs = rows // 2
         return s // pairs + 1, s % pairs * 2 + 1
 
-    def multiply(s, slot):
+    total = depth * rows // 2
+
+    def ready(s):
         z, y = place(s)
-        got = jnp.dot(c_ref[...], terms[slot], preferred_element_type=jnp.float32)
+        for r in range(2):
+            prepare(z, y + r, r)
+
+    def store(s, got):
+        z, y = place(s)
         for r in range(2):
             o_ref[z - 1, y - 1 + r] = got[:, r * LANES : (r + 1) * LANES].astype(jnp.bfloat16)
 
-    def ready(s, slot):
-        z, y = place(s)
-        for r in range(2):
-            prepare(z, y + r, r)
-        fill(slot)
+    def step(s, carry):
+        ready(s)
 
-    total = depth * rows // 2
-    ready(0, 0)
+        def group(g, inner):
+            fill(0, g)
+            return inner
 
-    def step(h, carry):
-        s = h * 2
-        ready(s + 1, 1)
-        multiply(s, 0)
-        ready(jnp.minimum(s + 2, total - 1), 0)
-        multiply(s + 1, 1)
+        lax.fori_loop(0, coefs // GROUP, group, 0)
+        store(s, jnp.dot(c_ref[...], terms[0], preferred_element_type=jnp.float32))
         return carry
 
-    lax.fori_loop(0, total // 2, step, 0)
+    lax.fori_loop(0, total, step, 0)
 
 
 def per_device(mode_field, conductivity, triple_out, triple_in, triple_coef, triple_value):
@@ -148,7 +150,7 @@
             pltpu.VMEM((2, 6, LANES, LANES), jnp.bfloat16),
             pltpu.VMEM((2, 6, coefs_pad, LANES), jnp.float32),
             pltpu.VMEM((2, 6, coefs, 16, LANES), jnp.bfloat16),
-            pltpu.VMEM((2, coefs * LANES, 2 * LANES), jnp.bfloat16),
+            pltpu.VMEM((1, coefs * LANES, 2 * LANES), jnp.bfloat16),
         ],
         compiler_params=pltpu.CompilerParams(vmem_limit_bytes=48 << 20),
     )(coupling, m_ext, k_ext)

time: 227 us -> 223 us (0.982)
  Pallas kernels: 187 us -> 182 us
    pallas_call x1, Pallas kernels: 177 us -> 172 us  [per_device(): pl.pallas_call(functools.partial(main_kernel, coefs, modes, depth, rows),...]
where the time goes in v1:
time: 223 us; the launch traced here: 222 us
  Pallas kernels  182 us (82%)
  local copies, waits for them, and re-layouts  15.8 us (7%)
  waiting for transfers between devices  11.4 us (5%)
  starting transfers between devices  11.3 us (5%)
    pallas_call x1, Pallas kernels, per_device(): pl.pallas_call(functools.partial(main_kernel, coefs, modes, depth, rows),...  172 us
    ppermute x2, waiting for transfers between devices, extend(): after = lax.ppermute(shard[:, :1], 'tile', down)  11.4 us
    pallas_call x1, Pallas kernels, coupling_matrix(): pl.pallas_call(functools.partial(coupling_kernel, coefs, modes), out_shap...  10.3 us
    ppermute x2, starting transfers between devices, extend(): before = lax.ppermute(shard[:, -1:], 'tile', up)  7.48 us
    unnamed x12, local copies, waits for them, and re-layouts  5.45 us
    transpose x1, local copies, waits for them, and re-layouts, per_device(): return jnp.transpose(out, (2, 0, 1, 3))  5.06 us
    pad x2, local copies, waits for them, and re-layouts, extend(): return jnp.pad(whole, ((0, 0), (1, 1), (0, pad), (0, 0)))  5.05 us
  transfers between devices with their start and end apart: 4, of which 1 were waited for; matrix products, arithmetic and copies ran while one was open for 1% of the time, Pallas kernels for 5%

profile of v1, /device:TPU:25, one launch (start us, length us, event | category | flops | bytes accessed | tf_op | source)
XLA Modules:
  0.0 222.3 jit_solution(16531681995921755071)
XLA Ops:
  0.0 4.6 %copy.7 = bf16[120,4,32,128]{3,0,2,1:T(8,128)(2,1)S(1)} copy(bf16[120,4,32,128]{3,2,1,0:T(8,128)(2,1)} %param.6) | data formatting | bytes 7864320 | tf_op args[0]
  4.6 0.0 copy-start.2
  4.7 0.0 copy-start.3
  4.7 0.0 copy-start.4
  4.7 0.0 copy-start
  4.7 0.0 copy-start.1
  4.7 0.1 fusion
  4.9 3.8 %collective-permute-start = (bf16[120,1,32,128]{3,0,2,1:T(8,128)(2,1)S(1)}, bf16[120,1,32,128]{3,0,2,1:T(8,128)(2,1)S(1)}, u32[]{:S(2)}, u32[]{:S(2)}) collective-permute-start(bf16[120,1,32,128]{3,0,2,1:T(8,128)(2,1)S(1)} %get-tuple-element.5), channel_id=1, source_target_pairs={{0,1},{1,2},{2,3},{3,4},{4,5},{5,6},{6,7},{7,8},{8,9},{9,10},{10,1... | collective-permute-start | bytes 2949128 | tf_op jit(solution)/shard_map/ppermute | solution.py:135
  8.7 1.9 collective-permute-start.1
  10.6 0.0 copy-done.2
  10.6 0.8 copy.10
  11.4 0.1 fusion.1
  11.5 3.6 %collective-permute-start.2 = (bf16[36,1,32,128]{3,0,2,1:T(8,128)(2,1)S(1)}, bf16[36,1,32,128]{3,0,2,1:T(8,128)(2,1)S(1)}, u32[]{:S(2)}, u32[]{:S(2)}) collective-permute-start(bf16[36,1,32,128]{3,0,2,1:T(8,128)(2,1)S(1)} %get-tuple-element.7), channel_id=1, source_target_pairs={{0,1},{1,2},{2,3},{3,4},{4,5},{5,6},{6,7},{7,8},{8,9},{9,10},{10,1... | collective-permute-start | bytes 884744 | tf_op jit(solution)/shard_map/ppermute | solution.py:135
  15.1 1.9 collective-permute-start.3
  17.1 0.0 copy-done.3
  17.1 0.0 copy-done.4
  17.1 0.0 copy-done
  17.1 0.0 copy-done.1
  17.1 10.3 %shard_map.64.c_ref = bf16[120,4608]{1,0:T(8,128)(2,1)S(1)} custom-call(s32[4096]{0:T(1024)S(1)} %multiply_add_fusion.row_ref, s32[4096]{0:T(1024)S(1)} %copy-done, f32[4096]{0:T(1024)S(1)} %copy-done.1), custom_call_target="tpu_custom_call" | custom-call | flops 40000000 | bytes 40000000 | tf_op jit(solution)/shard_map/pallas_call | solution.py:41
  27.4 0.0 collective-permute-done.2
  27.4 11.4 %collective-permute-done.3 = bf16[36,1,32,128]{3,0,2,1:T(8,128)(2,1)S(1)} collective-permute-done((bf16[36,1,32,128]{3,0,2,1:T(8,128)(2,1)S(1)}, bf16[36,1,32,128]{3,0,2,1:T(8,128)(2,1)S(1)}, u32[]{:S(2)}, u32[]{:S(2)}) %collective-permute-start.3) | collective-permute-done | bytes 294944 | tf_op jit(solution)/shard_map/ppermute | solution.py:136
  38.8 0.3 maximum_bitcast_fusion.1
  39.1 0.4 pad.9.k_ref
  39.5 0.0 collective-permute-done
  39.5 0.0 collective-permute-done.1
  39.5 0.9 maximum_bitcast_fusion
  40.4 4.6 %pad.8.m_ref = bf16[6,34,128,128]{3,2,1,0:T(8,128)(2,1)} pad(bf16[6,32,120,128]{3,2,1,0:T(8,128)(2,1)S(1)} %maximum_bitcast_fusion, bf16[]{:T(256)} %constant.4.clone.1), padding=0_0x1_1x0_8x0_0 | pad | bytes 12582914 | tf_op jit(solution)/shard_map/jit(_pad)/pad | solution.py:139
  45.1 172.2 %shard_map.65 = bf16[4,32,120,128]{3,2,1,0:T(8,128)(2,1)} custom-call(bf16[120,4608]{1,0:T(8,128)(2,1)S(1)} %shard_map.64.c_ref, bf16[6,34,128,128]{3,2,1,0:T(8,128)(2,1)} %pad.8.m_ref, bf16[6,34,48,128]{3,2,1,0:T(8,128)(2,1)S(1)} %pad.9.k_ref), custom_call_target="tpu_custom_call" | custom-call | tf_op jit(solution)/shard_map/pallas_call | solution.py:144
  217.3 5.1 %copy.13 = bf16[120,4,32,128]{3,2,1,0:T(8,128)(2,1)} copy(bf16[120,4,32,128]{3,0,2,1:T(8,128)(2,1)} %bitcast.5) | data formatting | bytes 7864320 | tf_op jit(solution)/shard_map/transpose | solution.py:157
  (1 shorter events, 0.0 us)
Async XLA Ops:
  4.6 6.0 %copy-start.2 = (bf16[36,4,32,128]{3,2,1,0:T(8,128)(2,1)S(1)}, bf16[36,4,32,128]{3,2,1,0:T(8,128)(2,1)}, u32[]{:S(2)}) copy-start(bf16[36,4,32,128]{3,2,1,0:T(8,128)(2,1)} %param.7) | copy-start | bytes 3538948
  4.7 12.4 %copy-start.3 = (s32[4096]{0:T(1024)S(1)}, s32[4096]{0:T(1024)}, u32[]{:S(2)}) copy-start(s32[4096]{0:T(1024)} %param.8) | copy-start | bytes 49156
  4.7 12.4 %copy-start.4 = (s32[4096]{0:T(1024)S(1)}, s32[4096]{0:T(1024)}, u32[]{:S(2)}) copy-start(s32[4096]{0:T(1024)} %param.10) | copy-start | bytes 49156
  4.7 12.4 %copy-start = (s32[4096]{0:T(1024)S(1)}, s32[4096]{0:T(1024)}, u32[]{:S(2)}) copy-start(s32[4096]{0:T(1024)} %in_ref.1) | copy-start | bytes 49156
  4.7 12.4 %copy-start.1 = (f32[4096]{0:T(1024)S(1)}, f32[4096]{0:T(1024)}, u32[]{:S(2)}) copy-start(f32[4096]{0:T(1024)} %value_ref.1) | copy-start | bytes 49156
  4.9 34.7 %collective-permute-start = (bf16[120,1,32,128]{3,0,2,1:T(8,128)(2,1)S(1)}, bf16[120,1,32,128]{3,0,2,1:T(8,128)(2,1)S(1)}, u32[]{:S(2)}, u32[]{:S(2)}) collective-permute-start(bf16[120,1,32,128]{3,0,2,1:T(8,128)(2,1)S(1)} %get-tuple-element.5), channel_id=1, source_target_pairs={{0,1},{1,2},{2,3},{3,4},{4,5},{5,6},{6,7},{7,8},{8,9},{9,10},{10,1... | collective-permute-start | bytes 2949128 | tf_op jit(solution)/shard_map/ppermute | solution.py:135
  8.7 30.8 %collective-permute-start.1 = (bf16[120,1,32,128]{3,0,2,1:T(8,128)(2,1)S(1)}, bf16[120,1,32,128]{3,0,2,1:T(8,128)(2,1)S(1)}, u32[]{:S(2)}, u32[]{:S(2)}) collective-permute-start(bf16[120,1,32,128]{3,0,2,1:T(8,128)(2,1)S(1)} %get-tuple-element.6), channel_id=1, source_target_pairs={{1,0},{2,1},{3,2},{4,3},{5,4},{6,5},{7,6},{8,7},{9,8},{10,9},{11,1... | collective-permute-start | bytes 2949128 | tf_op jit(solution)/shard_map/ppermute | solution.py:136
  11.5 15.9 %collective-permute-start.2 = (bf16[36,1,32,128]{3,0,2,1:T(8,128)(2,1)S(1)}, bf16[36,1,32,128]{3,0,2,1:T(8,128)(2,1)S(1)}, u32[]{:S(2)}, u32[]{:S(2)}) collective-permute-start(bf16[36,1,32,128]{3,0,2,1:T(8,128)(2,1)S(1)} %get-tuple-element.7), channel_id=1, source_target_pairs={{0,1},{1,2},{2,3},{3,4},{4,5},{5,6},{6,7},{7,8},{8,9},{9,10},{10,1... | collective-permute-start | bytes 884744 | tf_op jit(solution)/shard_map/ppermute | solution.py:135
  15.1 23.7 %collective-permute-start.3 = (bf16[36,1,32,128]{3,0,2,1:T(8,128)(2,1)S(1)}, bf16[36,1,32,128]{3,0,2,1:T(8,128)(2,1)S(1)}, u32[]{:S(2)}, u32[]{:S(2)}) collective-permute-start(bf16[36,1,32,128]{3,0,2,1:T(8,128)(2,1)S(1)} %get-tuple-element.8), channel_id=1, source_target_pairs={{1,0},{2,1},{3,2},{4,3},{5,4},{6,5},{7,6},{8,7},{9,8},{10,9},{11,1... | collective-permute-start | bytes 884744 | tf_op jit(solution)/shard_map/ppermute | solution.py:136

commit v2 on v1

--- a/solution.py
+++ b/solution.py
@@ -49,7 +49,31 @@
     )(rows, triple_in, triple_value)
 
 
-def main_kernel(coefs, modes, depth, rows, c_ref, m_ref, k_ref, o_ref, dm, kf, kb, terms):
+def assemble(ref, whole, before, after, depth, rows):
+    pad = ref.shape[2] - whole.shape[2]
+    blank = jnp.zeros(ref.shape[2:], ref.dtype)
+    for z in range(depth + 2):
+        ref[z, 0] = blank
+        ref[z, rows + 1] = blank
+
+    def widen(v):
+        edge = jnp.zeros((pad, v.shape[1]), jnp.float32)
+        return jnp.concatenate([v.astype(jnp.float32), edge], axis=0).astype(ref.dtype)
+
+    def row(y, carry):
+        ref[0, y + 1] = widen(before[0, y])
+        ref[depth + 1, y + 1] = widen(after[0, y])
+        for z in range(depth):
+            ref[z + 1, y + 1] = widen(whole[z, y])
+        return carry
+
+    lax.fori_loop(0, rows, row, 0)
+
+
+def main_kernel(coefs, modes, depth, rows, c_ref, m_in, m_before, m_after, k_in, k_before, k_after, o_ref, m_ref, k_ref, dm, kf, kb, terms):
+    for ref, whole, before, after in ((m_ref, m_in, m_before, m_after), (k_ref, k_in, k_before, k_after)):
+        assemble(ref, whole, before, after, depth, rows)
+
     lane = lax.broadcasted_iota(jnp.int32, (1, LANES), 1)
 
     def shifted(v):
@@ -131,29 +155,29 @@
     up = [(i, i + 1) for i in range(devices - 1)]
     down = [(j, i) for i, j in up]
 
-    def extend(shard, pad):
+    def extend(shard):
         before = lax.ppermute(shard[:, -1:], "tile", up)
         after = lax.ppermute(shard[:, :1], "tile", down)
-        whole = jnp.concatenate([before, shard, after], axis=1)
-        whole = jnp.transpose(whole, (1, 2, 0, 3))
-        return jnp.pad(whole, ((0, 0), (1, 1), (0, pad), (0, 0)))
+        return [jnp.transpose(part, (1, 2, 0, 3)) for part in (shard, before, after)]
 
-    m_ext = extend(mode_field, LANES - modes)
-    k_ext = extend(conductivity, coefs_pad - coefs)
+    m_parts = extend(mode_field)
+    k_parts = extend(conductivity)
     vmem = pl.BlockSpec(memory_space=pltpu.VMEM)
     out = pl.pallas_call(
         functools.partial(main_kernel, coefs, modes, depth, rows),
         out_shape=jax.ShapeDtypeStruct((depth, rows, modes, lanes), jnp.bfloat16),
-        in_specs=[vmem] * 3,
+        in_specs=[vmem] * 7,
         out_specs=vmem,
         scratch_shapes=[
+            pltpu.VMEM((depth + 2, rows + 2, LANES, lanes), jnp.bfloat16),
+            pltpu.VMEM((depth + 2, rows + 2, coefs_pad, lanes), jnp.bfloat16),
             pltpu.VMEM((2, 6, LANES, LANES), jnp.bfloat16),
             pltpu.VMEM((2, 6, coefs_pad, LANES), jnp.float32),
             pltpu.VMEM((2, 6, coefs, 16, LANES), jnp.bfloat16),
             pltpu.VMEM((1, coefs * LANES, 2 * LANES), jnp.bfloat16),
         ],
         compiler_params=pltpu.CompilerParams(vmem_limit_bytes=48 << 20),
-    )(coupling, m_ext, k_ext)
+    )(coupling, *m_parts, *k_parts)
     return jnp.transpose(out, (2, 0, 1, 3))
 
 

time: 223 us -> 215 us (0.964)
  waiting for transfers between devices: 11.4 us -> 6.31 us
  local copies, waits for them, and re-layouts: 15.8 us -> 13.3 us
    ppermute x2, waiting for transfers between devices: 11.4 us -> 6.31 us  [extend(): after = lax.ppermute(shard[:, :1], 'tile', down)]
    pad x2 -> x0, local copies, waits for them, and re-layouts: 5.05 us -> none  [extend(): return jnp.pad(whole, ((0, 0), (1, 1), (0, pad), (0, 0)))]
    unnamed x12 -> x18, local copies, waits for them, and re-layouts: 5.45 us -> 6.27 us
  transfers between devices with their start and end apart: 4 -> 4, of which waited for: 1 -> 1; matrix products, arithmetic and copies ran while one was open for 1% -> 3% of each run, Pallas kernels for 5% -> 5%
where the time goes in v2:
time: 215 us
  Pallas kernels  184 us (86%)
  local copies, waits for them, and re-layouts  13.3 us (6%)
  starting transfers between devices  11.5 us (5%)
  waiting for transfers between devices  6.31 us (3%)
    pallas_call x1, Pallas kernels, per_device(): pl.pallas_call(functools.partial(main_kernel, coefs, modes, depth, rows),...  174 us
    pallas_call x1, Pallas kernels, coupling_matrix(): pl.pallas_call(functools.partial(coupling_kernel, coefs, modes), out_shap...  10.3 us
    ppermute x2, starting transfers between devices, extend(): before = lax.ppermute(shard[:, -1:], 'tile', up)  7.61 us
    ppermute x2, waiting for transfers between devices, extend(): after = lax.ppermute(shard[:, :1], 'tile', down)  6.31 us
    unnamed x18, local copies, waits for them, and re-layouts  6.27 us
    transpose x1, local copies, waits for them, and re-layouts, per_device(): return jnp.transpose(out, (2, 0, 1, 3))  5.06 us
  transfers between devices with their start and end apart: 4, of which 1 were waited for; matrix products, arithmetic and copies ran while one was open for 3% of the time, Pallas kernels for 5%

profile of v2, /device:TPU:25, one launch (start us, length us, event | category | flops | bytes accessed | tf_op | source)
XLA Modules:
  0.0 215.2 jit_solution(9745850882140605558)
XLA Ops:
  0.0 0.0 copy-start.3
  0.0 2.0 fusion
  2.0 0.4 copy.16
  2.3 0.0 copy-start.2
  2.4 4.0 %collective-permute-start = (bf16[120,1,32,128]{3,0,2,1:T(8,128)(2,1)S(1)}, bf16[120,1,32,128]{3,0,2,1:T(8,128)(2,1)S(1)}, u32[]{:S(2)}, u32[]{:S(2)}) collective-permute-start(bf16[120,1,32,128]{3,0,2,1:T(8,128)(2,1)S(1)} %copy.16), channel_id=1, source_target_pairs={{0,1},{1,2},{2,3},{3,4},{4,5},{5,6},{6,7},{7,8},{8,9},{9,10},{10,1... | collective-permute-start | bytes 2949128 | tf_op jit(solution)/shard_map/ppermute | solution.py:159
  6.3 0.4 copy.17
  6.7 1.9 collective-permute-start.1
  8.7 0.0 copy-done.3
  8.7 0.1 copy.18
  8.8 3.6 %collective-permute-start.2 = (bf16[36,1,32,128]{3,0,2,1:T(8,128)(2,1)S(1)}, bf16[36,1,32,128]{3,0,2,1:T(8,128)(2,1)S(1)}, u32[]{:S(2)}, u32[]{:S(2)}) collective-permute-start(bf16[36,1,32,128]{3,0,2,1:T(8,128)(2,1)S(1)} %copy.18), channel_id=1, source_target_pairs={{0,1},{1,2},{2,3},{3,4},{4,5},{5,6},{6,7},{7,8},{8,9},{9,10},{10,1... | collective-permute-start | bytes 884744 | tf_op jit(solution)/shard_map/ppermute | solution.py:159
  12.5 0.1 copy.19
  12.6 1.9 collective-permute-start.3
  14.6 0.8 copy.20
  15.3 0.0 copy-done.2
  15.3 0.0 copy-start.4
  15.4 0.0 copy-start.5
  15.4 0.0 copy-start
  15.4 0.0 copy-start.1
  15.4 4.5 %copy.21 = bf16[120,4,32,128]{3,0,2,1:T(8,128)(2,1)} copy(bf16[120,4,32,128]{3,2,1,0:T(8,128)(2,1)S(1)} %copy-done.2) | data formatting | bytes 7864320 | tf_op args[0]
  19.9 0.0 copy-done.4
  19.9 0.0 copy-done.5
  19.9 0.0 copy-done
  19.9 0.0 copy-done.1
  19.9 10.3 %shard_map.64.c_ref = bf16[120,4608]{1,0:T(8,128)(2,1)S(1)} custom-call(s32[4096]{0:T(1024)S(1)} %multiply_add_fusion.row_ref, s32[4096]{0:T(1024)S(1)} %copy-done, f32[4096]{0:T(1024)S(1)} %copy-done.1), custom_call_target="tpu_custom_call" | custom-call | flops 40000000 | bytes 40000000 | tf_op jit(solution)/shard_map/pallas_call | solution.py:41
  30.2 0.0 collective-permute-done.2
  30.2 6.3 %collective-permute-done.3 = bf16[36,1,32,128]{3,0,2,1:T(8,128)(2,1)S(1)} collective-permute-done((bf16[36,1,32,128]{3,0,2,1:T(8,128)(2,1)S(1)}, bf16[36,1,32,128]{3,0,2,1:T(8,128)(2,1)S(1)}, u32[]{:S(2)}, u32[]{:S(2)}) %collective-permute-start.3) | collective-permute-done | bytes 294944 | tf_op jit(solution)/shard_map/ppermute | solution.py:160
  36.5 0.0 collective-permute-done
  36.5 0.0 collective-permute-done.1
  36.5 173.7 %shard_map.65 = bf16[4,32,120,128]{3,2,1,0:T(8,128)(2,1)} custom-call(bf16[120,4608]{1,0:T(8,128)(2,1)S(1)} %shard_map.64.c_ref, bf16[4,32,120,128]{3,2,1,0:T(8,128)(2,1)} %bitcast.16, bf16[1,32,120,128]{3,2,1,0:T(8,128)(2,1)S(1)} %bitcast.12, bf16[1,32,120,128]{3,2,1,0:T(8,128)(2,1)S(1)} %bitcast.13, bf16[4,32,36,128]{3,2,1,0:T(8,128)(2,1)S(1)} %bitcast.11, ...), custom_call_target="tpu_custom_call" | custom-call | tf_op jit(solution)/shard_map/pallas_call | solution.py:166
  210.2 5.1 %copy.13 = bf16[120,4,32,128]{3,2,1,0:T(8,128)(2,1)} copy(bf16[120,4,32,128]{3,0,2,1:T(8,128)(2,1)} %bitcast.17) | data formatting | bytes 7864320 | tf_op jit(solution)/shard_map/transpose | solution.py:181
  (2 shorter events, 0.0 us)
Async XLA Ops:
  0.0 8.7 %copy-start.3 = (bf16[36,4,32,128]{3,2,1,0:T(8,128)(2,1)S(1)}, bf16[36,4,32,128]{3,2,1,0:T(8,128)(2,1)}, u32[]{:S(2)}) copy-start(bf16[36,4,32,128]{3,2,1,0:T(8,128)(2,1)} %param.7) | copy-start | bytes 3538948
  2.3 13.0 %copy-start.2 = (bf16[120,4,32,128]{3,2,1,0:T(8,128)(2,1)S(1)}, bf16[120,4,32,128]{3,2,1,0:T(8,128)(2,1)}, u32[]{:S(2)}) copy-start(bf16[120,4,32,128]{3,2,1,0:T(8,128)(2,1)} %param.6) | copy-start | bytes 11796484
  2.4 34.1 %collective-permute-start = (bf16[120,1,32,128]{3,0,2,1:T(8,128)(2,1)S(1)}, bf16[120,1,32,128]{3,0,2,1:T(8,128)(2,1)S(1)}, u32[]{:S(2)}, u32[]{:S(2)}) collective-permute-start(bf16[120,1,32,128]{3,0,2,1:T(8,128)(2,1)S(1)} %copy.16), channel_id=1, source_target_pairs={{0,1},{1,2},{2,3},{3,4},{4,5},{5,6},{6,7},{7,8},{8,9},{9,10},{10,1... | collective-permute-start | bytes 2949128 | tf_op jit(solution)/shard_map/ppermute | solution.py:159
  6.7 29.8 %collective-permute-start.1 = (bf16[120,1,32,128]{3,0,2,1:T(8,128)(2,1)S(1)}, bf16[120,1,32,128]{3,0,2,1:T(8,128)(2,1)S(1)}, u32[]{:S(2)}, u32[]{:S(2)}) collective-permute-start(bf16[120,1,32,128]{3,0,2,1:T(8,128)(2,1)S(1)} %copy.17), channel_id=1, source_target_pairs={{1,0},{2,1},{3,2},{4,3},{5,4},{6,5},{7,6},{8,7},{9,8},{10,9},{11,1... | collective-permute-start | bytes 2949128 | tf_op jit(solution)/shard_map/ppermute | solution.py:160
  8.8 21.3 %collective-permute-start.2 = (bf16[36,1,32,128]{3,0,2,1:T(8,128)(2,1)S(1)}, bf16[36,1,32,128]{3,0,2,1:T(8,128)(2,1)S(1)}, u32[]{:S(2)}, u32[]{:S(2)}) collective-permute-start(bf16[36,1,32,128]{3,0,2,1:T(8,128)(2,1)S(1)} %copy.18), channel_id=1, source_target_pairs={{0,1},{1,2},{2,3},{3,4},{4,5},{5,6},{6,7},{7,8},{8,9},{9,10},{10,1... | collective-permute-start | bytes 884744 | tf_op jit(solution)/shard_map/ppermute | solution.py:159
  12.6 23.9 %collective-permute-start.3 = (bf16[36,1,32,128]{3,0,2,1:T(8,128)(2,1)S(1)}, bf16[36,1,32,128]{3,0,2,1:T(8,128)(2,1)S(1)}, u32[]{:S(2)}, u32[]{:S(2)}) collective-permute-start(bf16[36,1,32,128]{3,0,2,1:T(8,128)(2,1)S(1)} %copy.19), channel_id=1, source_target_pairs={{1,0},{2,1},{3,2},{4,3},{5,4},{6,5},{7,6},{8,7},{9,8},{10,9},{11,1... | collective-permute-start | bytes 884744 | tf_op jit(solution)/shard_map/ppermute | solution.py:160
  15.3 4.5 %copy-start.4 = (s32[4096]{0:T(1024)S(1)}, s32[4096]{0:T(1024)}, u32[]{:S(2)}) copy-start(s32[4096]{0:T(1024)} %param.8) | copy-start | bytes 49156
  15.4 4.5 %copy-start.5 = (s32[4096]{0:T(1024)S(1)}, s32[4096]{0:T(1024)}, u32[]{:S(2)}) copy-start(s32[4096]{0:T(1024)} %param.10) | copy-start | bytes 49156
  15.4 4.5 %copy-start = (s32[4096]{0:T(1024)S(1)}, s32[4096]{0:T(1024)}, u32[]{:S(2)}) copy-start(s32[4096]{0:T(1024)} %in_ref.1) | copy-start | bytes 49156
  15.4 4.5 %copy-start.1 = (f32[4096]{0:T(1024)S(1)}, f32[4096]{0:T(1024)}, u32[]{:S(2)}) copy-start(f32[4096]{0:T(1024)} %value_ref.1) | copy-start | bytes 49156

commit v3 on v2

--- a/solution.py
+++ b/solution.py
@@ -8,7 +8,7 @@
 
 LANES = 128
 COPIES = 4
-GROUP = 6
+GROUP = 12
 
 
 def coupling_kernel(coefs, modes, row_ref, in_ref, value_ref, out_ref, *sums):

time: 215 us -> 215 us (level)
  no operation moved by 1% of the time
where the time goes in v3:
time: 215 us
  Pallas kernels  184 us (86%)
  local copies, waits for them, and re-layouts  13.3 us (6%)
  starting transfers between devices  11.5 us (5%)
  waiting for transfers between devices  6.31 us (3%)
    pallas_call x1, Pallas kernels, per_device(): pl.pallas_call(functools.partial(main_kernel, coefs, modes, depth, rows),...  173 us
    pallas_call x1, Pallas kernels, coupling_matrix(): pl.pallas_call(functools.partial(coupling_kernel, coefs, modes), out_shap...  10.3 us
    ppermute x2, starting transfers between devices, extend(): before = lax.ppermute(shard[:, -1:], 'tile', up)  7.61 us
    ppermute x2, waiting for transfers between devices, extend(): after = lax.ppermute(shard[:, :1], 'tile', down)  6.31 us
    unnamed x18, local copies, waits for them, and re-layouts  6.27 us
    transpose x1, local copies, waits for them, and re-layouts, per_device(): return jnp.transpose(out, (2, 0, 1, 3))  5.06 us
  transfers between devices with their start and end apart: 4, of which 1 were waited for; matrix products, arithmetic and copies ran while one was open for 3% of the time, Pallas kernels for 5%

profile of v3, /device:TPU:25, one launch (start us, length us, event | category | flops | bytes accessed | tf_op | source)
XLA Modules:
  0.0 214.9 jit_solution(9455409078471946012)
XLA Ops:
  0.0 0.0 copy-start.3
  0.0 2.0 fusion
  2.0 0.4 copy.16
  2.3 0.0 copy-start.2
  2.4 4.0 %collective-permute-start = (bf16[120,1,32,128]{3,0,2,1:T(8,128)(2,1)S(1)}, bf16[120,1,32,128]{3,0,2,1:T(8,128)(2,1)S(1)}, u32[]{:S(2)}, u32[]{:S(2)}) collective-permute-start(bf16[120,1,32,128]{3,0,2,1:T(8,128)(2,1)S(1)} %copy.16), channel_id=1, source_target_pairs={{0,1},{1,2},{2,3},{3,4},{4,5},{5,6},{6,7},{7,8},{8,9},{9,10},{10,1... | collective-permute-start | bytes 2949128 | tf_op jit(solution)/shard_map/ppermute | solution.py:159
  6.3 0.4 copy.17
  6.7 1.9 collective-permute-start.1
  8.7 0.0 copy-done.3
  8.7 0.1 copy.18
  8.8 3.6 %collective-permute-start.2 = (bf16[36,1,32,128]{3,0,2,1:T(8,128)(2,1)S(1)}, bf16[36,1,32,128]{3,0,2,1:T(8,128)(2,1)S(1)}, u32[]{:S(2)}, u32[]{:S(2)}) collective-permute-start(bf16[36,1,32,128]{3,0,2,1:T(8,128)(2,1)S(1)} %copy.18), channel_id=1, source_target_pairs={{0,1},{1,2},{2,3},{3,4},{4,5},{5,6},{6,7},{7,8},{8,9},{9,10},{10,1... | collective-permute-start | bytes 884744 | tf_op jit(solution)/shard_map/ppermute | solution.py:159
  12.5 0.1 copy.19
  12.6 1.9 collective-permute-start.3
  14.6 0.8 copy.20
  15.3 0.0 copy-done.2
  15.3 0.0 copy-start.4
  15.4 0.0 copy-start.5
  15.4 0.0 copy-start
  15.4 0.0 copy-start.1
  15.4 4.5 %copy.21 = bf16[120,4,32,128]{3,0,2,1:T(8,128)(2,1)} copy(bf16[120,4,32,128]{3,2,1,0:T(8,128)(2,1)S(1)} %copy-done.2) | data formatting | bytes 7864320 | tf_op args[0]
  19.9 0.0 copy-done.4
  19.9 0.0 copy-done.5
  19.9 0.0 copy-done
  19.9 0.0 copy-done.1
  19.9 10.3 %shard_map.64.c_ref = bf16[120,4608]{1,0:T(8,128)(2,1)S(1)} custom-call(s32[4096]{0:T(1024)S(1)} %multiply_add_fusion.row_ref, s32[4096]{0:T(1024)S(1)} %copy-done, f32[4096]{0:T(1024)S(1)} %copy-done.1), custom_call_target="tpu_custom_call" | custom-call | flops 40000000 | bytes 40000000 | tf_op jit(solution)/shard_map/pallas_call | solution.py:41
  30.2 0.0 collective-permute-done.2
  30.2 6.3 %collective-permute-done.3 = bf16[36,1,32,128]{3,0,2,1:T(8,128)(2,1)S(1)} collective-permute-done((bf16[36,1,32,128]{3,0,2,1:T(8,128)(2,1)S(1)}, bf16[36,1,32,128]{3,0,2,1:T(8,128)(2,1)S(1)}, u32[]{:S(2)}, u32[]{:S(2)}) %collective-permute-start.3) | collective-permute-done | bytes 294944 | tf_op jit(solution)/shard_map/ppermute | solution.py:160
  36.5 0.0 collective-permute-done
  36.5 0.0 collective-permute-done.1
  36.5 173.3 %shard_map.65 = bf16[4,32,120,128]{3,2,1,0:T(8,128)(2,1)} custom-call(bf16[120,4608]{1,0:T(8,128)(2,1)S(1)} %shard_map.64.c_ref, bf16[4,32,120,128]{3,2,1,0:T(8,128)(2,1)} %bitcast.16, bf16[1,32,120,128]{3,2,1,0:T(8,128)(2,1)S(1)} %bitcast.12, bf16[1,32,120,128]{3,2,1,0:T(8,128)(2,1)S(1)} %bitcast.13, bf16[4,32,36,128]{3,2,1,0:T(8,128)(2,1)S(1)} %bitcast.11, ...), custom_call_target="tpu_custom_call" | custom-call | tf_op jit(solution)/shard_map/pallas_call | solution.py:166
  209.8 5.1 %copy.13 = bf16[120,4,32,128]{3,2,1,0:T(8,128)(2,1)} copy(bf16[120,4,32,128]{3,0,2,1:T(8,128)(2,1)} %bitcast.17) | data formatting | bytes 7864320 | tf_op jit(solution)/shard_map/transpose | solution.py:181
  (2 shorter events, 0.0 us)
Async XLA Ops:
  0.0 8.7 %copy-start.3 = (bf16[36,4,32,128]{3,2,1,0:T(8,128)(2,1)S(1)}, bf16[36,4,32,128]{3,2,1,0:T(8,128)(2,1)}, u32[]{:S(2)}) copy-start(bf16[36,4,32,128]{3,2,1,0:T(8,128)(2,1)} %param.7) | copy-start | bytes 3538948
  2.3 13.0 %copy-start.2 = (bf16[120,4,32,128]{3,2,1,0:T(8,128)(2,1)S(1)}, bf16[120,4,32,128]{3,2,1,0:T(8,128)(2,1)}, u32[]{:S(2)}) copy-start(bf16[120,4,32,128]{3,2,1,0:T(8,128)(2,1)} %param.6) | copy-start | bytes 11796484
  2.4 34.1 %collective-permute-start = (bf16[120,1,32,128]{3,0,2,1:T(8,128)(2,1)S(1)}, bf16[120,1,32,128]{3,0,2,1:T(8,128)(2,1)S(1)}, u32[]{:S(2)}, u32[]{:S(2)}) collective-permute-start(bf16[120,1,32,128]{3,0,2,1:T(8,128)(2,1)S(1)} %copy.16), channel_id=1, source_target_pairs={{0,1},{1,2},{2,3},{3,4},{4,5},{5,6},{6,7},{7,8},{8,9},{9,10},{10,1... | collective-permute-start | bytes 2949128 | tf_op jit(solution)/shard_map/ppermute | solution.py:159
  6.7 29.8 %collective-permute-start.1 = (bf16[120,1,32,128]{3,0,2,1:T(8,128)(2,1)S(1)}, bf16[120,1,32,128]{3,0,2,1:T(8,128)(2,1)S(1)}, u32[]{:S(2)}, u32[]{:S(2)}) collective-permute-start(bf16[120,1,32,128]{3,0,2,1:T(8,128)(2,1)S(1)} %copy.17), channel_id=1, source_target_pairs={{1,0},{2,1},{3,2},{4,3},{5,4},{6,5},{7,6},{8,7},{9,8},{10,9},{11,1... | collective-permute-start | bytes 2949128 | tf_op jit(solution)/shard_map/ppermute | solution.py:160
  8.8 21.3 %collective-permute-start.2 = (bf16[36,1,32,128]{3,0,2,1:T(8,128)(2,1)S(1)}, bf16[36,1,32,128]{3,0,2,1:T(8,128)(2,1)S(1)}, u32[]{:S(2)}, u32[]{:S(2)}) collective-permute-start(bf16[36,1,32,128]{3,0,2,1:T(8,128)(2,1)S(1)} %copy.18), channel_id=1, source_target_pairs={{0,1},{1,2},{2,3},{3,4},{4,5},{5,6},{6,7},{7,8},{8,9},{9,10},{10,1... | collective-permute-start | bytes 884744 | tf_op jit(solution)/shard_map/ppermute | solution.py:159
  12.6 23.9 %collective-permute-start.3 = (bf16[36,1,32,128]{3,0,2,1:T(8,128)(2,1)S(1)}, bf16[36,1,32,128]{3,0,2,1:T(8,128)(2,1)S(1)}, u32[]{:S(2)}, u32[]{:S(2)}) collective-permute-start(bf16[36,1,32,128]{3,0,2,1:T(8,128)(2,1)S(1)} %copy.19), channel_id=1, source_target_pairs={{1,0},{2,1},{3,2},{4,3},{5,4},{6,5},{7,6},{8,7},{9,8},{10,9},{11,1... | collective-permute-start | bytes 884744 | tf_op jit(solution)/shard_map/ppermute | solution.py:160
  15.3 4.5 %copy-start.4 = (s32[4096]{0:T(1024)S(1)}, s32[4096]{0:T(1024)}, u32[]{:S(2)}) copy-start(s32[4096]{0:T(1024)} %param.8) | copy-start | bytes 49156
  15.4 4.5 %copy-start.5 = (s32[4096]{0:T(1024)S(1)}, s32[4096]{0:T(1024)}, u32[]{:S(2)}) copy-start(s32[4096]{0:T(1024)} %param.10) | copy-start | bytes 49156
  15.4 4.5 %copy-start = (s32[4096]{0:T(1024)S(1)}, s32[4096]{0:T(1024)}, u32[]{:S(2)}) copy-start(s32[4096]{0:T(1024)} %in_ref.1) | copy-start | bytes 49156
  15.4 4.5 %copy-start.1 = (f32[4096]{0:T(1024)S(1)}, f32[4096]{0:T(1024)}, u32[]{:S(2)}) copy-start(f32[4096]{0:T(1024)} %value_ref.1) | copy-start | bytes 49156
